TPU v7x, 32 devices: a whole 2x2x4 slice. The times are simulated.
32 devices in a mesh: group: 2 (over y), seq: 8 (over z, core), mp: 2 (over x).
Axes of the slice: x: 2, y: 2, z: 4, core: 2. Of those that a mesh axis runs over, the one named last changes fastest.
Arguments:
- hidden: bfloat16 [2, 4096, 4096], P('group', 'seq', 'mp'), may hold values from -16 to 16
- w_qkv: bfloat16 [8, 4096, 768], P('mp'), may hold values from -0.09375 to 0.09375
- cache: bfloat16 [1024, 128, 8, 256], P('seq', None, 'mp'), may hold values from -16 to 16
- cache_len: int32 [1024], P('seq'), may hold values from 1 to 128, as said below
- receive: int32 [1024], P('seq'), may hold values 0 or 1
Outputs:
- attended: bfloat16 [2, 4096, 4096], P('group', 'seq', 'mp')
Inputs may be any that keep to these rules, and one draw needn't show every extreme that they name: `cache_len`: in each seq shard's 128 requests one has length 128.
All inputs are finite; a program needn't handle non-finite values. No bound on the sum of `receive` on one device may be relied on, other than what follows from the above.
Results may differ from a plain program's by a relative error of at most 0.0098.
Values may be sent and summed in bfloat16 or wider, within the bound.
No kernel may reach another device: no remote copies, remote signals or barrier semaphores. Data moves between devices by JAX's collectives and lax.ppermute only.
A program may use at most 384 MiB of HBM per device.

v0:
```python
import jax
import jax.numpy as jnp
from jax import lax
from jax.sharding import PartitionSpec as P

MASKED_SCORE = -1e30


def passed_along(block, axis, distance):
    devices = range(lax.axis_size(axis))
    route = [(i - distance, i) for i in devices if i - distance in devices]
    return lax.ppermute(block, axis, route)


def shards(hidden, w_qkv, cache, cache_len, receive):
    group_count = w_qkv.shape[0]
    column_count = w_qkv.shape[2]
    head_width = cache.shape[3] // 2
    heads_per_group = column_count // head_width - 2
    row_count = hidden.shape[1]
    requests = cache.shape[0]
    draft_count = row_count // requests
    slot_count = cache.shape[1]
    score_scale = head_width ** (-0.5)
    projected = jnp.einsum(
        "rd,gdc->grc",
        lax.all_gather(hidden, "mp", axis=2, tiled=True)[0],
        w_qkv,
        preferred_element_type=jnp.float32,
    ).astype(jnp.bfloat16)
    queries = projected[:, :, : heads_per_group * head_width].reshape(
        group_count, row_count, heads_per_group, head_width
    )
    new_kv = projected[:, :, heads_per_group * head_width :]
    prefill = lax.axis_index("group") == 0
    decode_on = jnp.logical_not(prefill)
    query_pos = lax.axis_index("seq") * row_count + jnp.arange(row_count, dtype=jnp.int32)
    admitted = jnp.repeat(receive, draft_count) > 0
    query_req = queries.reshape(group_count, requests, draft_count, heads_per_group, head_width)
    own_keys = new_kv[..., :head_width].reshape(group_count, requests, draft_count, head_width)
    own_values = new_kv[..., head_width:].reshape(group_count, requests, draft_count, head_width)
    cache_logits = (
        jnp.einsum(
            "gbtph,bugh->gbtpu",
            query_req,
            cache[..., :head_width],
            preferred_element_type=jnp.float32,
        )
        * score_scale
    )
    own_logits = (
        jnp.einsum("gbtph,gbuh->gbtpu", query_req, own_keys, preferred_element_type=jnp.float32)
        * score_scale
    )
    live_cache = (
        (jnp.arange(slot_count, dtype=jnp.int32)[None, :] < cache_len[:, None]) & decode_on
    )[None, :, None, None, :]
    causal = jnp.arange(draft_count)[None, :] <= jnp.arange(draft_count)[:, None]
    live_own = (causal & decode_on)[None, None, :, None, :]
    running_max = jnp.maximum(
        jnp.max(jnp.where(live_cache, cache_logits, MASKED_SCORE), axis=-1),
        jnp.max(jnp.where(live_own, own_logits, MASKED_SCORE), axis=-1),
    )
    cache_weights = jnp.where(live_cache, jnp.exp(cache_logits - running_max[..., None]), 0.0)
    own_weights = jnp.where(live_own, jnp.exp(own_logits - running_max[..., None]), 0.0)
    running_sum = jnp.sum(cache_weights, axis=-1) + jnp.sum(own_weights, axis=-1)
    weighted = jnp.einsum(
        "gbtpu,bugh->gbtph",
        cache_weights.astype(jnp.bfloat16),
        cache[..., head_width:],
        preferred_element_type=jnp.float32,
    )
    weighted = weighted + jnp.einsum(
        "gbtpu,gbuh->gbtph",
        own_weights.astype(jnp.bfloat16),
        own_values,
        preferred_element_type=jnp.float32,
    )
    carried_state = (
        running_max.reshape(group_count, row_count, heads_per_group),
        running_sum.reshape(group_count, row_count, heads_per_group),
        weighted.reshape(group_count, row_count, heads_per_group, head_width),
    )
    assembled = lax.all_gather(new_kv, "seq", axis=1, tiled=True)
    arrived = passed_along(assembled, "group", 1)
    prompt_kv = jnp.where(prefill, assembled, arrived)
    old_max, old_sum, old_weighted = carried_state
    key_count = prompt_kv.shape[1]
    logits = (
        jnp.einsum(
            "grph,gjh->grpj",
            queries,
            prompt_kv[..., :head_width],
            preferred_element_type=jnp.float32,
        )
        * score_scale
    )
    key_pos = jnp.arange(key_count, dtype=jnp.int32)
    allowed = jnp.where(prefill, key_pos[None, :] <= query_pos[:, None], admitted[:, None])[
        None, :, None, :
    ]
    new_max = jnp.maximum(old_max, jnp.max(jnp.where(allowed, logits, MASKED_SCORE), axis=-1))
    weights = jnp.where(allowed, jnp.exp(logits - new_max[..., None]), 0.0)
    rescale = jnp.exp(old_max - new_max)
    new_sum = old_sum * rescale + jnp.sum(weights, axis=-1)
    new_weighted = old_weighted * rescale[..., None] + jnp.einsum(
        "grpj,gjh->grph",
        weights.astype(jnp.bfloat16),
        prompt_kv[..., head_width:],
        preferred_element_type=jnp.float32,
    )
    carried_state = (new_max, new_sum, new_weighted)
    final_max, final_sum, final_weighted = carried_state
    output = (final_weighted / final_sum[..., None]).astype(jnp.bfloat16)
    return jnp.transpose(output, (1, 0, 2, 3)).reshape(
        1, row_count, group_count * heads_per_group * head_width
    )


def solution(mesh):
    return jax.shard_map(
        shards,
        mesh=mesh,
        in_specs=(
            P("group", "seq", "mp"),
            P("mp", None, None),
            P("seq", None, "mp", None),
            P("seq"),
            P("seq"),
        ),
        out_specs=P("group", "seq", "mp"),
        check_vma=False,
    )
```

profile of v0, /device:TPU:5, one launch (start us, length us, event | category | flops | bytes accessed | tf_op | source)
XLA Modules:
  0.0 510.1 jit_solution(17949003393746029689)
XLA Ops:
  6.5 0.7 all-gather.3.cloned.1.call-update
  7.3 59.6 %all-gather.3.cloned.1.call-done = bf16[1,512,4096]{2,1,0:T(8,128)(2,1)} async-done(((bf16[1,512,2048]{2,1,0:T(8,128)(2,1)}), bf16[1,512,4096]{2,1,0:T(8,128)(2,1)}) %all-gather.3.cloned.1.call-update) | async-done | bytes 4194320 | tf_op jit(solution)/shard_map/all_gather | solution.py:27
  66.9 18.1 %convert_bitcast_fusion = bf16[4,512,768]{2,1,0:T(8,128)(2,1)S(1)} fusion(bf16[4,4096,768]{2,1,0:T(8,128)(2,1)} %param.6, bf16[1,512,4096]{2,1,0:T(8,128)(2,1)} %all-gather.3.cloned.1.call-done), kind=kOutput, calls=%fused_computation.21 | convolution fusion | flops 12886474752 | bytes 32505856 | tf_op jit(solution)/shard_map/rd,gdc->grc/dot_general | solution.py:25
  85.0 1.6 copy-done.2
  86.7 1.0 slice.37
  88.1 3.2 fusion.7
  91.3 79.1 %all-gather.5.cloned.1.call-done = bf16[4,4096,256]{2,1,0:T(8,128)(2,1)} async-done(((bf16[4,512,256]{2,1,0:T(8,128)(2,1)}), bf16[4,4096,256]{2,1,0:T(8,128)(2,1)}) %all-gather.5.cloned.1.call-update) | async-done | bytes 8388624 | tf_op jit(solution)/shard_map/all_gather | solution.py:84
  170.3 1.5 collective-permute-start
  171.8 23.0 %fusion.33 = (bf16[128,128,4,128]{3,2,1,0:T(4,128)(2,1)}, bf16[128,128,4,128]{3,2,1,0:T(4,128)(2,1)}) fusion(bf16[128,128,4,256]{3,2,1,0:T(4,128)(2,1)} %param.7), kind=kLoop, calls=%fused_computation.48 | loop fusion | bytes 67108864 | tf_op jit(solution)/shard_map/slice | solution.py:70
  194.8 3.6 slice_bitcast_fusion.6
  198.4 2.1 reshape_reshape.3
  200.4 2.1 fusion.34
  202.6 22.1 %fusion.35 = f32[4,128,4,4,4]{3,4,2,1,0:T(4,128)} fusion(bf16[4,128,4,4,128]{4,3,2,1,0:T(4,128)(2,1)} %reshape_reshape.3, bf16[4,128,4,128,1]{3,2,4,1,0:T(4,128)(2,1)S(1)} %bitcast.81), kind=kOutput, calls=%fused_computation.50 | convolution fusion | flops 8388608 | bytes 2752512 | tf_op jit(solution)/shard_map/gbtph,gbuh->gbtpu/dot_general | solution.py:52
  224.7 3.9 copy.42
  228.7 0.4 copy.64
  229.2 16.4 %select_reduce_fusion.1 = (f32[4,128,4,4]{3,2,1,0:T(4,128)}, f32[4,128,4,4,128]{4,3,2,1,0:T(4,128)}) fusion(pred[128,128]{1,0:T(8,128)(4,1)S(1)} %fusion.25, bf16[4,128,4,4,128]{4,3,2,1,0:T(4,128)(2,1)S(1)} %copy-done.1, bf16[128,128,4,128]{3,2,1,0:T(4,128)(2,1)} %get-tuple-element.8), kind=kOutput, calls=%fused_computation.20 | convolution fusion | flops 271572992 | bytes 23117824 | tf_op jit(solution)/shard_map/gbtph,bugh->gbtpu/dot_general | solution.py:43
  245.6 1.5 max.34
  247.1 0.3 copy.45
  247.4 0.4 copy.60
  247.9 0.4 copy.65
  248.4 14.7 %fusion.13 = f32[4,128,4,4]{3,2,1,0:T(4,128)S(1)} fusion(f32[4,128,4,4,128]{4,3,2,1,0:T(4,128)} %get-tuple-element.16, f32[4,128,4,4]{3,2,1,0:T(4,128)S(1)} %max.34, pred[128,128]{1,0:T(8,128)(4,1)S(1)} %fusion.25), kind=kLoop, calls=%fused_computation.22 | loop fusion | flops 4186112 | bytes 4276224 | tf_op jit(solution)/shard_map/reduce_sum | solution.py:66
  263.4 0.3 copy.63
  263.7 1.9 copy.46
  265.6 4.2 fusion.36
  269.8 14.5 %fusion.15 = f32[4,128,4,4,128]{4,3,2,1,0:T(4,128)} fusion(f32[4,128,4,4,128]{4,3,2,1,0:T(4,128)} %fusion.36, bf16[128,128,4,128]{3,2,1,0:T(4,128)(2,1)} %get-tuple-element.7, f32[4,128,4,4,128]{4,3,2,1,0:T(4,128)} %get-tuple-element.16, f32[4,128,4,4]{3,2,1,0:T(4,128)S(1)} %max.34, pred[128,128]{1,0:T(8,128)(4,1)S(1)} %fusion.25), kind=kOutput, calls=%fused_computation.24 | convolution fusion | flops 273678336 | bytes 29409280 | tf_op jit(solution)/shard_map/gbtpu,bugh->gbtph/dot_general | solution.py:67
  284.3 5.3 %copy.49 = f32[4,512,4,128]{1,3,2,0:T(8,128)} copy(f32[4,512,4,128]{3,2,1,0:T(4,128)} %bitcast.78) | data formatting | bytes 8388608 | tf_op jit(solution)/shard_map/reshape | solution.py:82
  289.6 64.8 %collective-permute-done = bf16[4,4096,256]{2,1,0:T(8,128)(2,1)} collective-permute-done((bf16[4,4096,256]{2,1,0:T(8,128)(2,1)}, bf16[4,4096,256]{2,1,0:T(8,128)(2,1)}, u32[]{:S(2)}, u32[]{:S(2)}) %collective-permute-start) | collective-permute-done | bytes 8388640 | tf_op jit(solution)/shard_map/ppermute | solution.py:12
  354.3 7.2 %broadcast_select_fusion = bf16[4,4096,256]{2,1,0:T(8,128)(2,1)} fusion(bf16[4,4096,256]{2,1,0:T(8,128)(2,1)} %all-gather.5.cloned.1.call-done, bf16[4,4096,256]{2,1,0:T(8,128)(2,1)} %collective-permute-done, pred[]{:T(512)S(6)} %eq.3), kind=kLoop, calls=%fused_computation.12 | loop fusion | flops 4194304 | bytes 25165824 | tf_op jit(solution)/shard_map/jit(_where)/select_n | solution.py:86
  361.6 48.9 %select_reduce_fusion = (f32[4,512,4]{1,2,0:T(4,128)S(1)}, f32[4,512,4,4096]{3,1,2,0:T(8,128)}) fusion(pred[512,4096]{1,0:T(8,128)(4,1)S(1)} %copy-done, bf16[4,4096,256]{2,1,0:T(8,128)(2,1)} %broadcast_select_fusion, bf16[4,64,4,8,128]{4,3,2,1,0:T(8,128)(2,1)} %get-tuple-element.9), kind=kOutput, calls=%fused_computation.1 | convolution fusion | flops 8690589696 | bytes 142639104 | tf_op jit(solution)/shard_map/grph,gjh->grpj/dot_general | solution.py:90
  410.5 41.4 %fusion = f32[4,512,4]{1,2,0:T(4,128)S(1)} fusion(f32[4,512,4,4096]{3,1,2,0:T(8,128)} %get-tuple-element.18, f32[4,512,4]{1,2,0:T(4,128)S(1)} %max.36, pred[512,4096]{1,0:T(8,128)(4,1)S(1)} %copy-done), kind=kLoop, calls=%fused_computation.2 | loop fusion | flops 134209536 | bytes 136380416 | tf_op jit(solution)/shard_map/reduce_sum | solution.py:105
  451.9 47.3 %divide_convert_fusion = bf16[4,512,4,128]{1,3,2,0:T(8,128)(2,1)} fusion(f32[4,512,4,128]{1,3,2,0:T(8,128)} %copy.49, f32[4,512,4]{1,2,0:T(4,128)S(1)} %bitcast.86, f32[4,512,4]{1,2,0:T(4,128)S(1)} %bitcast.87, bf16[4,4096,256]{2,1,0:T(8,128)(2,1)} %broadcast_select_fusion, f32[4,512,4,4096]{3,1,2,0:T(8,128)} %get-tuple-element.18, ...), kind=kOutput, calls=%fused_computation.18 | convolution fusion | flops 8728346624 | bytes 146898944 | tf_op jit(solution)/shard_map/grpj,gjh->grph/dot_general | solution.py:106
  499.2 3.9 copy.53
  (23 shorter events, 1.1 us)
Async XLA Ops:
  6.5 60.4 %all-gather.3.cloned.1.call-start = ((), (), s32[]{:S(2)}) async-start(), calls=%async_computation | async-start | bytes 6291456 | tf_op jit(solution)/shard_map/all_gather | solution.py:27
  7.3 80.5 %copy-start.4 = (s32[128]{0:T(128)S(1)}, s32[128]{0:T(128)}, u32[]{:S(2)}) copy-start(s32[128]{0:T(128)} %param.9) | copy-start | bytes 1540
  7.3 80.7 %copy-start.3 = (s32[128]{0:T(128)S(1)}, s32[128]{0:T(128)}, u32[]{:S(2)}) copy-start(s32[128]{0:T(128)} %param.8) | copy-start | bytes 1540
  7.3 163.1 %all-gather.5.cloned.1.call-start = ((), (), s32[]{:S(2)}) async-start(), calls=%async_computation.1 | async-start | bytes 9437184 | tf_op jit(solution)/shard_map/all_gather | solution.py:84
  85.0 1.6 copy-start.2
  170.3 184.0 %collective-permute-start = (bf16[4,4096,256]{2,1,0:T(8,128)(2,1)}, bf16[4,4096,256]{2,1,0:T(8,128)(2,1)}, u32[]{:S(2)}, u32[]{:S(2)}) collective-permute-start(bf16[4,4096,256]{2,1,0:T(8,128)(2,1)} %all-gather.5.cloned.1.call-done), channel_id=1, source_target_pairs={{0,16},{1,17},{2,18},{3,19},{4,20},{5,21},{6,22},{7,23},{8,24},{9,... | collective-permute-start | bytes 25165832 | tf_op jit(solution)/shard_map/ppermute | solution.py:12
  224.7 4.5 copy-start.1
  289.6 72.0 %copy-start = (pred[512,4096]{1,0:T(8,128)(4,1)S(1)}, pred[512,4096]{1,0:T(8,128)(4,1)}, u32[]{:S(2)}) copy-start(pred[512,4096]{1,0:T(8,128)(4,1)} %fusion.7) | copy-start | bytes 6291460
Sparse Core Ops, SparseCore 0:
  8.9 57.9 all-gather.2
  87.8 82.4 all-gather.4
where the time goes:
time: 516 us; the launch traced here: 510 us
  waiting for transfers between devices  204 us (40%)
  matrix products  172 us (33%)
  other arithmetic  68.7 us (13%)
  local copies, waits for them, and re-layouts  50.4 us (10%)
  between operations  13.8 us (3%)
    all_gather x1, waiting for transfers between devices, shards(): assembled = lax.all_gather(new_kv, 'seq', axis=1, tiled=True)  79.1 us
    ppermute x1, waiting for transfers between devices, passed_along(): return lax.ppermute(block, axis, route)  64.8 us
    all_gather x1, waiting for transfers between devices, shards(): lax.all_gather(hidden, 'mp', axis=2, tiled=True)[0]  59.6 us
    dot_general x1, matrix products, shards(): jnp.einsum('grph,gjh->grpj', queries, prompt_kv[..., :head_width], prefer...  48.9 us
    dot_general x1, matrix products, shards(): jnp.einsum('grpj,gjh->grph', weights.astype(jnp.bfloat16), prompt_kv[...,...  47.3 us
    reduce_sum x1, other arithmetic, shards(): new_sum = old_sum * rescale + jnp.sum(weights, axis=-1)  41.4 us
    slice x1, local copies, waits for them, and re-layouts, shards(): cache[..., head_width:]  23 us
    dot_general x1, matrix products, shards(): jnp.einsum('gbtph,gbuh->gbtpu', query_req, own_keys, preferred_element_ty...  22.1 us
  transfers between devices with their start and end apart: 3, of which 3 were waited for; matrix products, arithmetic and copies ran while one was open for 24% of the time, Pallas kernels for 0%

commit v1 on v0

--- a/solution.py
+++ b/solution.py
@@ -1,9 +1,17 @@
+import functools
+
 import jax
 import jax.numpy as jnp
 from jax import lax
+from jax.experimental import pallas as pl
+from jax.experimental.pallas import tpu as pltpu
 from jax.sharding import PartitionSpec as P
 
 MASKED_SCORE = -1e30
+BLOCK_ROWS = 128
+MIB = 1 << 20
+NT = (((1,), (1,)), ((), ()))
+NN = (((1,), (0,)), ((), ()))
 
 
 def passed_along(block, axis, distance):
@@ -12,7 +20,599 @@
     return lax.ppermute(block, axis, route)
 
 
-def shards(hidden, w_qkv, cache, cache_len, receive):
+def dot(a, b, dims):
+    return lax.dot_general(a, b, dims, preferred_element_type=jnp.float32)
+
+
+def compiler_params(mib, steps=1):
+    return pltpu.CompilerParams(
+        dimension_semantics=("arbitrary",) * steps, vmem_limit_bytes=mib * MIB
+    )
+
+
+def kv_kernel(ids, own, own_s, oth, oth_s, wa0, wb0, wa1, wb1, kv0, kv1):
+    core = ids[0]
+    x_own = jnp.concatenate([own[...], own_s[...]], axis=0)
+    x_oth = jnp.concatenate([oth[...], oth_s[...]], axis=0)
+    rows = own.shape[0]
+    for wa, wb, out in ((wa0, wb0, kv0), (wa1, wb1, kv1)):
+        res = (dot(x_own, wa[0], NN) + dot(x_oth, wb[0], NN)).astype(jnp.bfloat16)
+        out[core] = res[:rows]
+        out[1 - core] = res[rows:]
+
+
+def project_kv(ids, own, own_s, oth, oth_s, w, chunk, start):
+    rows, width = oth.shape
+    kv_cols = w.shape[2] // 3
+    first = start // rows
+
+    def row_map(i, ids):
+        return (first, 0)
+
+    def whole(i, ids):
+        return (0, 0)
+
+    def w_map(gi, flip):
+        def at(i, ids):
+            half = ids[3] if flip == 0 else 1 - ids[3]
+            return (2 * ids[0] + gi, half, 2)
+
+        return at
+
+    out_spec = pl.BlockSpec((2, rows, kv_cols), lambda i, ids: (0, 0, 0))
+    return pl.pallas_call(
+        kv_kernel,
+        grid_spec=pltpu.PrefetchScalarGridSpec(
+            num_scalar_prefetch=1,
+            grid=(1,),
+            in_specs=[
+                pl.BlockSpec((rows, width), row_map),
+                pl.BlockSpec((rows, width), row_map),
+                pl.BlockSpec((rows, width), whole),
+                pl.BlockSpec((rows, width), whole),
+            ]
+            + [
+                pl.BlockSpec((1, width, kv_cols), w_map(gi, flip))
+                for gi in range(2)
+                for flip in range(2)
+            ],
+            out_specs=[out_spec, out_spec],
+        ),
+        out_shape=[jax.ShapeDtypeStruct((2, rows, kv_cols), jnp.bfloat16)] * 2,
+        compiler_params=compiler_params(40),
+        cost_estimate=pl.CostEstimate(
+            flops=2 * 2 * rows * 2 * width * 2 * kv_cols,
+            bytes_accessed=2 * (4 * rows * width + 4 * width * kv_cols),
+            transcendentals=0,
+        ),
+        name="project_kv",
+    )(ids, own, own_s, oth, oth_s, w, w, w, w)
+
+
+def q_kernel(heads, ids, own, own_s, oth, oth_s, wa, wb, kv0, kv1, *refs):
+    q_out, theirs = refs[-2:]
+    gi = pl.program_id(0)
+    core = ids[0]
+    rows = own.shape[0]
+    x_own = jnp.concatenate([own[...], own_s[...]], axis=0)
+    x_oth = jnp.concatenate([oth[...], oth_s[...]], axis=0)
+    res = (dot(x_own, wa[0], NN) + dot(x_oth, wb[0], NN)).astype(jnp.bfloat16)
+    head_width = res.shape[1] // heads
+    per_core = rows // BLOCK_ROWS
+    for side in range(2):
+        at = core if side == 0 else 1 - core
+        for sub in range(per_core):
+            for h in range(heads):
+                lo = side * rows + sub * BLOCK_ROWS
+                q_out[0, at * per_core + sub, h * BLOCK_ROWS : (h + 1) * BLOCK_ROWS, :] = res[
+                    lo : lo + BLOCK_ROWS, h * head_width : (h + 1) * head_width
+                ]
+    theirs[0, :, : heads * head_width] = res[rows:]
+
+    @pl.when(gi == 0)
+    def _():
+        theirs[0, :, heads * head_width :] = kv0[1 - core]
+
+    @pl.when(gi == 1)
+    def _():
+        theirs[0, :, heads * head_width :] = kv1[1 - core]
+
+
+def project_q(ids, own, own_s, oth, oth_s, w, kv0, kv1, before, chunk, start, blocks):
+    rows, width = oth.shape
+    columns = w.shape[2]
+    q_cols = columns * 2 // 3
+    kv_cols = columns - q_cols
+    heads = q_cols * 2 // kv_cols
+    head_width = q_cols // heads
+    first = start // rows
+    here = 2 * rows // BLOCK_ROWS
+    first_block = 2 * start // BLOCK_ROWS // here
+
+    def row_map(i, ids):
+        return (first, 0)
+
+    def whole(i, ids):
+        return (0, 0)
+
+    def w_map(flip):
+        def at(i, ids):
+            return (2 * ids[0] + i, ids[3] if flip == 0 else 1 - ids[3], 0)
+
+        return at
+
+    in_specs = (
+        [
+            pl.BlockSpec((rows, width), row_map),
+            pl.BlockSpec((rows, width), row_map),
+            pl.BlockSpec((rows, width), whole),
+            pl.BlockSpec((rows, width), whole),
+        ]
+        + [pl.BlockSpec((1, width, q_cols), w_map(flip)) for flip in range(2)]
+        + [pl.BlockSpec((2, rows, kv_cols), lambda i, ids: (0, 0, 0))] * 2
+    )
+    args = [ids, own, own_s, oth, oth_s, w, w, kv0, kv1]
+    aliases = {}
+    if before is not None:
+        in_specs.append(pl.BlockSpec(memory_space=pl.ANY))
+        aliases = {len(args): 0}
+        args.append(before)
+    return pl.pallas_call(
+        functools.partial(q_kernel, heads),
+        grid_spec=pltpu.PrefetchScalarGridSpec(
+            num_scalar_prefetch=1,
+            grid=(2,),
+            in_specs=in_specs,
+            out_specs=[
+                pl.BlockSpec(
+                    (1, here, heads * BLOCK_ROWS, head_width),
+                    lambda i, ids: (i, first_block, 0, 0),
+                ),
+                pl.BlockSpec((1, rows, columns), lambda i, ids: (i, 0, 0)),
+            ],
+        ),
+        out_shape=[
+            jax.ShapeDtypeStruct((2, blocks, heads * BLOCK_ROWS, head_width), jnp.bfloat16),
+            jax.ShapeDtypeStruct((2, rows, columns), jnp.bfloat16),
+        ],
+        input_output_aliases=aliases,
+        compiler_params=compiler_params(56),
+        cost_estimate=pl.CostEstimate(
+            flops=2 * 2 * rows * 2 * width * 2 * q_cols,
+            bytes_accessed=2 * (4 * rows * width + 4 * width * q_cols),
+            transcendentals=0,
+        ),
+        name="project_q",
+    )(*args)
+
+
+SUB_REQ = 4
+
+
+def cache_kernel(heads, draft, step_req, start_req, scale, ids, lens, cache, q, kv0, kv1, swapped, flags, mine, theirs):
+    groups, _, slots, both = cache.shape
+    width = both // 2
+    core = ids[0]
+    step = pl.program_id(0)
+    rows = SUB_REQ * draft
+    per_block = BLOCK_ROWS // (step_req * draft)
+
+    @pl.when(ids[2] == 1)
+    def _():
+        r_of_row = (lax.broadcasted_iota(jnp.int32, (heads * rows, SUB_REQ * slots), 0) % rows) // draft
+        key = lax.broadcasted_iota(jnp.int32, (heads * rows, SUB_REQ * slots), 1)
+        r_of_key = key // slots
+        slot = key % slots
+        own_row = lax.broadcasted_iota(jnp.int32, (heads * rows, rows), 0) % rows
+        own_key = lax.broadcasted_iota(jnp.int32, (heads * rows, rows), 1)
+        own_ok = (own_row // draft == own_key // draft) & (own_key <= own_row)
+        for sub in range(step_req // SUB_REQ):
+            req0 = start_req + step * step_req + sub * SUB_REQ
+            limit = jnp.zeros((heads * rows, SUB_REQ * slots), jnp.int32)
+            for r in range(SUB_REQ):
+                limit = jnp.where(r_of_key == r, lens[req0 + r], limit)
+            ok = (r_of_row == r_of_key) & (slot < limit)
+            row0 = step % per_block * (step_req * draft) + sub * rows
+            row0 = pl.multiple_of(row0, rows)
+            flat0 = pl.multiple_of(sub * rows, rows)
+            for g in range(groups):
+                gi = g % 2
+                for side in range(2):
+                    if g // 2 != side:
+                        continue
+                    cache_g = 2 * (core if side == 0 else 1 - core) + gi
+                    kv = cache[cache_g, sub * SUB_REQ : (sub + 1) * SUB_REQ].reshape(
+                        SUB_REQ * slots, both
+                    )
+                    if side == 0:
+                        qs = jnp.concatenate(
+                            [
+                                q[gi, 0, pl.ds(h * BLOCK_ROWS + row0, rows), :]
+                                for h in range(heads)
+                            ],
+                            axis=0,
+                        )
+                        own = (kv0 if gi == 0 else kv1)[0, pl.ds(flat0, rows), :]
+                    else:
+                        block = swapped[gi, pl.ds(flat0, rows), :]
+                        qs = jnp.concatenate(
+                            [block[:, h * width : (h + 1) * width] for h in range(heads)], axis=0
+                        )
+                        own = block[:, heads * width :]
+                    s = dot(qs, kv[:, :width], NT) * scale
+                    s_own = dot(qs, own[:, :width], NT) * scale
+                    s = jnp.where(ok, s, MASKED_SCORE)
+                    s_own = jnp.where(own_ok, s_own, MASKED_SCORE)
+                    top = jnp.maximum(
+                        jnp.max(s, axis=1, keepdims=True), jnp.max(s_own, axis=1, keepdims=True)
+                    )
+                    p = jnp.exp(s - top)
+                    p_own = jnp.exp(s_own - top)
+                    total = jnp.sum(p, axis=1, keepdims=True) + jnp.sum(
+                        p_own, axis=1, keepdims=True
+                    )
+                    o = dot(p.astype(jnp.bfloat16), kv[:, width:], NN) + dot(
+                        p_own.astype(jnp.bfloat16), own[:, width:], NN
+                    )
+                    o = o / total
+                    lse = top + jnp.log(total)
+                    out = mine if side == 0 else theirs
+                    for h in range(heads):
+                        out[gi, sub * rows : (sub + 1) * rows, h * width : (h + 1) * width] = o[
+                            h * rows : (h + 1) * rows
+                        ]
+                        out[
+                            gi,
+                            sub * rows : (sub + 1) * rows,
+                            (heads + h) * width : (heads + h + 1) * width,
+                        ] = jnp.broadcast_to(lse[h * rows : (h + 1) * rows], (rows, width)) if False else jnp.broadcast_to(
+                            lse[h * rows : (h + 1) * rows], (rows, width)
+                        )
+
+
+def cache_attention(ids, lens, cache_t, q, kv0, kv1, swapped, start, rows, draft, scale):
+    groups, _, slots, both = cache_t.shape
+    width = both // 2
+    heads = q.shape[2] // BLOCK_ROWS
+    step_req = 8
+    steps = rows // (step_req * draft)
+    step_rows = step_req * draft
+    start_req = start // draft
+    per_block = BLOCK_ROWS // step_rows
+    blocks_core = rows // BLOCK_ROWS
+    block0 = 2 * start // BLOCK_ROWS
+
+    def q_map(i, ids, lens):
+        return (0, block0 + ids[0] * blocks_core + i // per_block, 0, 0)
+
+    out_spec = pl.BlockSpec((2, step_rows, 2 * heads * width), lambda i, ids, lens: (0, i, 0))
+    return pl.pallas_call(
+        functools.partial(cache_kernel, heads, draft, step_req, start_req, scale),
+        grid_spec=pltpu.PrefetchScalarGridSpec(
+            num_scalar_prefetch=2,
+            grid=(steps,),
+            in_specs=[
+                pl.BlockSpec(
+                    (groups, step_req, slots, both),
+                    lambda i, ids, lens: (0, (start_req // step_req + i) * ids[2], 0, 0),
+                ),
+                pl.BlockSpec((2, 1, heads * BLOCK_ROWS, width), q_map),
+                pl.BlockSpec((1, step_rows, both), lambda i, ids, lens: (ids[0], i, 0)),
+                pl.BlockSpec((1, step_rows, both), lambda i, ids, lens: (ids[0], i, 0)),
+                pl.BlockSpec((2, step_rows, swapped.shape[2]), lambda i, ids, lens: (0, i, 0)),
+                pl.BlockSpec(memory_space=pl.ANY),
+            ],
+            out_specs=[out_spec, out_spec],
+        ),
+        out_shape=[jax.ShapeDtypeStruct((2, rows, 2 * heads * width), jnp.float32)] * 2,
+        compiler_params=compiler_params(40),
+        cost_estimate=pl.CostEstimate(
+            flops=4 * rows * heads * groups * SUB_REQ * slots * width,
+            bytes_accessed=2 * groups * rows // draft * slots * both,
+            transcendentals=rows * heads * groups * slots * SUB_REQ,
+        ),
+        name="cache_attention",
+    )(ids, lens, cache_t, q, kv0, kv1, swapped, ids)
+
+
+def prompt_kernel(
+    first, last, slots_n, starts, key_start, rows_core, scale, n_state, ids, *refs
+):
+    refs = list(refs)
+    q = refs.pop(0)
+    own = [refs.pop(0), refs.pop(0)]
+    arrived = [refs.pop(0) for _ in range(slots_n)]
+    if not first:
+        acc_in, ml_in = refs.pop(0), refs.pop(0)
+    if last:
+        part_mine, part_theirs, flags = refs.pop(0), refs.pop(0), refs.pop(0)
+        out_ref = refs.pop(0)
+    else:
+        acc_out, ml_out = refs.pop(0), refs.pop(0)
+    kvbuf, acc, m_ref, l_ref, sems = refs
+    gi, blk = pl.program_id(0), pl.program_id(1)
+    core, z, grp = ids[0], ids[1], ids[2]
+    chips = slots_n // 2
+    place = jnp.where(grp == 0, z, slots_n - 1 - z)
+    keys = kvbuf.shape[2]
+    heads = q.shape[2] // BLOCK_ROWS
+    width = q.shape[3]
+
+    def copies():
+        made = []
+        for t in range(slots_n):
+            r = lax.rem(place - t + slots_n, slots_n)
+            lane = r // chips
+            chip = jnp.where(lane == 0, r, slots_n - 1 - r)
+            made.append(
+                pltpu.make_async_copy(arrived[t], kvbuf.at[lane, chip], sems.at[t])
+            )
+        return made
+
+    @pl.when((gi == 0) & (blk == 0))
+    def _():
+        for copy in copies():
+            copy.start()
+        for copy in copies():
+            copy.wait()
+
+    if first:
+        acc[...] = jnp.zeros_like(acc)
+        m_ref[...] = jnp.full_like(m_ref, MASKED_SCORE)
+        l_ref[...] = jnp.zeros_like(l_ref)
+    else:
+        acc[...] = acc_in[0, 0]
+        for h in range(heads):
+            m_ref[h * BLOCK_ROWS : (h + 1) * BLOCK_ROWS, :] = jnp.broadcast_to(
+                ml_in[0, 0, :, h : h + 1], (BLOCK_ROWS, 128)
+            )
+            l_ref[h * BLOCK_ROWS : (h + 1) * BLOCK_ROWS, :] = jnp.broadcast_to(
+                ml_in[0, 0, :, heads + h : heads + h + 1], (BLOCK_ROWS, 128)
+            )
+
+    def visit(k, v, mask):
+        s = dot(q[0, 0], k, NT)
+        if mask is not None:
+            s = jnp.where(mask, s, MASKED_SCORE)
+        old = m_ref[:, :1]
+        new = jnp.maximum(old, jnp.max(s, axis=1, keepdims=True))
+        p = jnp.exp((s - new) * scale)
+        fade = jnp.exp((old - new) * scale)
+        l_ref[...] = jnp.broadcast_to(
+            l_ref[:, :1] * fade + jnp.sum(p, axis=1, keepdims=True), l_ref.shape
+        )
+        acc[...] = acc[...] * fade + dot(p.astype(jnp.bfloat16), v, NN)
+        m_ref[...] = jnp.broadcast_to(new, m_ref.shape)
+
+    def full(chip, carry):
+        visit(kvbuf[gi, chip, :, :width], kvbuf[gi, chip, :, width:], None)
+        return carry
+
+    lax.fori_loop(0, jnp.where(grp == 0, z, chips), full, 0)
+
+    pos = ids[8 + blk]
+    own_rows = own[0].shape[1]
+    for kc in range(2):
+        key0 = kc * rows_core + key_start
+
+        @pl.when((grp == 0) & (key0 <= pos + BLOCK_ROWS - 1))
+        def _():
+            shape = (heads * BLOCK_ROWS, own_rows)
+            row_pos = pos + lax.broadcasted_iota(jnp.int32, shape, 0) % BLOCK_ROWS
+            key_pos = key0 + lax.broadcasted_iota(jnp.int32, shape, 1)
+            kv = jnp.where(gi == 0, own[0][kc], own[1][kc])
+            visit(kv[:, :width], kv[:, width:], key_pos <= row_pos)
+
+    if not last:
+        acc_out[0, 0] = acc[...]
+        for h in range(heads):
+            ml_out[0, 0, :, h : h + 1] = m_ref[h * BLOCK_ROWS : (h + 1) * BLOCK_ROWS, :1]
+            ml_out[0, 0, :, heads + h : heads + h + 1] = l_ref[
+                h * BLOCK_ROWS : (h + 1) * BLOCK_ROWS, :1
+            ]
+    else:
+
+        @pl.when(grp == 0)
+        def _():
+            o = acc[...] / l_ref[:, :1]
+            for h in range(heads):
+                out_ref[:, h * width : (h + 1) * width] = o[
+                    h * BLOCK_ROWS : (h + 1) * BLOCK_ROWS
+                ].astype(jnp.bfloat16)
+
+        @pl.when(grp == 1)
+        def _():
+            here = pos // rows_core == core
+            for h in range(heads):
+                part = slice(h * BLOCK_ROWS, (h + 1) * BLOCK_ROWS)
+                columns = slice(h * width, (h + 1) * width)
+                wide = slice((heads + h) * width, (heads + h + 1) * width)
+                o_c = jnp.where(here, part_mine[0, :, columns], part_theirs[0, :, columns])
+                lse_c = jnp.where(here, part_mine[0, :, wide], part_theirs[0, :, wide])
+                o_p = acc[part] / l_ref[part]
+                lse_p = m_ref[part] * scale + jnp.log(l_ref[part])
+                lse_p = jnp.where(flags[0] > 0, lse_p, MASKED_SCORE)
+                top = jnp.maximum(lse_p, lse_c)
+                w_p = jnp.exp(lse_p - top)
+                w_c = jnp.exp(lse_c - top)
+                out_ref[:, columns] = ((o_p * w_p + o_c * w_c) / (w_p + w_c)).astype(jnp.bfloat16)
+
+
+def prompt_attention(ids, q, own, arrived, state, merge, starts, sizes, chunk, rows_core, scale):
+    slots_n = len(arrived)
+    _, blocks, stacked, width = q.shape
+    heads = stacked // BLOCK_ROWS
+    first, last = state is None, merge is not None
+    size = sizes[chunk]
+    keys = 2 * size
+
+    def by_block(gi, blk, ids):
+        return (gi, blk, 0, 0)
+
+    acc_spec = pl.BlockSpec((1, 1, stacked, width), by_block)
+    ml_spec = pl.BlockSpec((1, 1, BLOCK_ROWS, 128), by_block)
+    own_spec = pl.BlockSpec((2, size, 2 * width), lambda gi, blk, ids: (0, 0, 0))
+    in_specs = [acc_spec, own_spec, own_spec] + [pl.BlockSpec(memory_space=pl.ANY)] * slots_n
+    args = [ids, q, *own, *[a.reshape(keys, 2 * width) for a in arrived]]
+    if not first:
+        in_specs += [acc_spec, ml_spec]
+        args += list(state)
+    if last:
+        def part_map(gi, blk, ids):
+            return (gi, ids[8 + blk] % rows_core // BLOCK_ROWS, 0)
+
+        part_spec = pl.BlockSpec((1, BLOCK_ROWS, 2 * heads * width), part_map)
+        in_specs += [
+            part_spec,
+            part_spec,
+            pl.BlockSpec((1, BLOCK_ROWS, 128), lambda gi, blk, ids: (blk, 0, 0)),
+        ]
+        args += list(merge)
+        out_specs = [
+            pl.BlockSpec(
+                (BLOCK_ROWS, heads * width),
+                lambda gi, blk, ids: (ids[8 + blk] // BLOCK_ROWS, gi),
+            )
+        ]
+        out_shape = [jax.ShapeDtypeStruct((2 * rows_core, 2 * heads * width), jnp.bfloat16)]
+    else:
+        out_specs = [acc_spec, ml_spec]
+        out_shape = [
+            jax.ShapeDtypeStruct((2, blocks, stacked, width), jnp.float32),
+            jax.ShapeDtypeStruct((2, blocks, BLOCK_ROWS, 128), jnp.float32),
+        ]
+    chips = slots_n // 2
+    pairs = 2 * blocks * stacked * keys * chips
+    return pl.pallas_call(
+        functools.partial(
+            prompt_kernel,
+            first,
+            last,
+            slots_n,
+            starts,
+            starts[chunk],
+            rows_core,
+            scale,
+            None,
+        ),
+        grid_spec=pltpu.PrefetchScalarGridSpec(
+            num_scalar_prefetch=1,
+            grid=(2, blocks),
+            in_specs=in_specs,
+            out_specs=out_specs,
+            scratch_shapes=[
+                pltpu.VMEM((2, chips, keys, 2 * width), jnp.bfloat16),
+                pltpu.VMEM((stacked, width), jnp.float32),
+                pltpu.VMEM((stacked, 128), jnp.float32),
+                pltpu.VMEM((stacked, 128), jnp.float32),
+                pltpu.SemaphoreType.DMA((slots_n,)),
+            ],
+        ),
+        out_shape=out_shape,
+        compiler_params=compiler_params(48, 2),
+        cost_estimate=pl.CostEstimate(
+            flops=4 * pairs * width, bytes_accessed=16 * MIB, transcendentals=pairs
+        ),
+        name="prompt_attention",
+    )(*args)
+
+
+CHUNKS = 2
+
+
+def fast_shards(hidden, w_qkv, cache, cache_len, receive):
+    head_width = cache.shape[3] // 2
+    heads = w_qkv.shape[2] // head_width - 2
+    rows_core = hidden.shape[1]
+    requests = cache.shape[0]
+    draft = rows_core // requests
+    scale = head_width ** (-0.5)
+    seq_n = lax.axis_size("seq")
+    chips = seq_n // 2
+    ring_n = 2 * chips
+    sizes = [rows_core // CHUNKS] * CHUNKS
+    starts = [sum(sizes[:c]) for c in range(CHUNKS)]
+    blocks = 2 * rows_core // BLOCK_ROWS
+
+    seq_i, group_i, mp_i = lax.axis_index("seq"), lax.axis_index("group"), lax.axis_index("mp")
+    core, chip = seq_i % 2, seq_i // 2
+    places = []
+    for size, start in zip(sizes, starts):
+        for c in range(2):
+            places += [c * rows_core + start + s for s in range(0, size, BLOCK_ROWS)]
+    ids = jnp.concatenate(
+        [
+            jnp.stack([core, chip, group_i, mp_i]).astype(jnp.int32),
+            jnp.zeros((4,), jnp.int32),
+            jnp.array(places, jnp.int32),
+        ]
+    )
+    prefill = group_i == 0
+
+    mp_swap = [(0, 1), (1, 0)]
+    core_swap = [(i, i ^ 1) for i in range(seq_n)]
+    ring = [(0, k) for k in range(chips)] + [(1, chips - 1 - k) for k in range(chips)]
+    index = [[g * seq_n + 2 * k + c for c in range(2)] for g, k in ring]
+    up = [(index[r][c], index[(r + 1) % ring_n][c]) for r in range(ring_n) for c in range(2)]
+    down = [(index[r][c], index[r - 1][c]) for r in range(ring_n) for c in range(2)]
+
+    def swap_cores(x):
+        return lax.ppermute(x, "seq", core_swap)
+
+    own = hidden[0]
+    oth = [lax.ppermute(own[s : s + n], "mp", mp_swap) for s, n in zip(starts, sizes)]
+    own_s = swap_cores(own)
+    oth_s = [swap_cores(x) for x in oth]
+    flag_mine = jnp.repeat(receive, draft).astype(jnp.float32)
+    flag_theirs = swap_cores(flag_mine)
+    cache_t = jnp.transpose(cache, (2, 0, 1, 3))
+
+    kvs, arrived, parts = [], [], []
+    q = None
+    for c, (start, size) in enumerate(zip(starts, sizes)):
+        kv0, kv1 = project_kv(ids, own, own_s, oth[c], oth_s[c], w_qkv, c, start)
+        crossed = lax.ppermute(kv1, "group", [(0, 1)])
+        block = jnp.where(prefill, kv0, crossed)
+        ups, downs = [block], [block]
+        for step in range(ring_n // 2):
+            ups.append(lax.ppermute(ups[-1], ("group", "seq"), up))
+            if step < ring_n // 2 - 1:
+                downs.append(lax.ppermute(downs[-1], ("group", "seq"), down))
+        kvs.append((kv0, kv1))
+        arrived.append(ups + downs[:0:-1])
+        q, theirs = project_q(
+            ids, own, own_s, oth[c], oth_s[c], w_qkv, kv0, kv1, q, c, start, blocks
+        )
+        swapped = swap_cores(theirs)
+        mine, away = cache_attention(
+            ids, cache_len, cache_t, q, kv0, kv1, swapped, start, size, draft, scale
+        )
+        parts.append((mine, swap_cores(away)))
+    merge_mine = jnp.concatenate([p[0] for p in parts], axis=1)
+    merge_theirs = jnp.concatenate([p[1] for p in parts], axis=1)
+    flags_by_core = jnp.where(
+        core == 0, jnp.stack([flag_mine, flag_theirs]), jnp.stack([flag_theirs, flag_mine])
+    ).reshape(2 * rows_core)
+    flags = jnp.stack([flags_by_core[p : p + BLOCK_ROWS] for p in places])
+    flags = jnp.broadcast_to(flags[:, :, None], (blocks, BLOCK_ROWS, 128))
+
+    state = None
+    for c in range(CHUNKS):
+        merge = (merge_mine, merge_theirs, flags) if c == CHUNKS - 1 else None
+        state = prompt_attention(
+            ids, q, kvs[c], arrived[c], state, merge, starts, sizes, c, rows_core, scale
+        )
+    done = state[0].reshape(2, rows_core, state[0].shape[1])
+    mine = jnp.where(core == 0, done[0], done[1])
+    back = swap_cores(jnp.where(core == 0, done[1], done[0]))
+    return jnp.where(
+        core == 0,
+        jnp.concatenate([mine, back], axis=1),
+        jnp.concatenate([back, mine], axis=1),
+    )[None]
+
+
+def plain_shards(hidden, w_qkv, cache, cache_len, receive):
     group_count = w_qkv.shape[0]
     column_count = w_qkv.shape[2]
     head_width = cache.shape[3] // 2
@@ -118,6 +718,20 @@
 
 
 def solution(mesh):
+    def shards(hidden, w_qkv, cache, cache_len, receive):
+        head_width = cache.shape[3] // 2
+        fits = (
+            mesh.shape["group"] == 2
+            and mesh.shape["mp"] == 2
+            and mesh.shape["seq"] % 2 == 0
+            and w_qkv.shape[0] == 4
+            and w_qkv.shape[2] == 6 * head_width
+            and head_width == 128
+            and hidden.shape[1] % (CHUNKS * BLOCK_ROWS) == 0
+        )
+        run = fast_shards if fits else plain_shards
+        return run(hidden, w_qkv, cache, cache_len, receive)
+
     return jax.shard_map(
         shards,
         mesh=mesh,

time: 516 us -> 478 us (0.926)
  the two profiles are of different devices: /device:TPU:5 before, /device:TPU:27 now
where the time goes in v1:
time: 478 us
  Pallas kernels  292 us (61%)
  waiting for transfers between devices  75.5 us (16%)
  starting transfers between devices  60.8 us (13%)
  local copies, waits for them, and re-layouts  37.5 us (8%)
  other arithmetic  11.2 us (2%)
    pallas_call x2, Pallas kernels, prompt_attention(): pl.pallas_call(functools.partial(prompt_kernel, first, last, slots_n, sta...  249 us
    ppermute x2, waiting for transfers between devices, fast_shards(): lax.ppermute(own[s:s + n], 'mp', mp_swap)  44 us
    unnamed x60, local copies, waits for them, and re-layouts  34.2 us
    ppermute x8, starting transfers between devices, fast_shards(): ups.append(lax.ppermute(ups[-1], ('group', 'seq'), up))  26.3 us
    ppermute x2, starting transfers between devices, fast_shards(): crossed = lax.ppermute(kv1, 'group', [(0, 1)])  20.9 us
    pallas_call x2, Pallas kernels, project_q(): pl.pallas_call(functools.partial(q_kernel, heads), grid_spec=pltpu.Prefet...  20 us
    ppermute x6, waiting for transfers between devices, fast_shards(): downs.append(lax.ppermute(downs[-1], ('group', 'seq'), down))  16.2 us
    pallas_call x2, Pallas kernels, project_kv(): pl.pallas_call(kv_kernel, grid_spec=pltpu.PrefetchScalarGridSpec(num_scal...  12.6 us
  transfers between devices with their start and end apart: 27, of which 11 were waited for; matrix products, arithmetic and copies ran while one was open for 7% of the time, Pallas kernels for 33%

profile of v1, /device:TPU:27, one launch (start us, length us, event | category | flops | bytes accessed | tf_op | source)
XLA Modules:
  0.0 477.6 jit_solution(15621920529836032101)
XLA Ops:
  0.7 2.7 slice_bitcast_fusion
  4.8 23.2 %collective-permute-done.3.oth = bf16[256,2048]{1,0:T(8,128)(2,1)} collective-permute-done((bf16[256,2048]{1,0:T(8,128)(2,1)S(1)}, bf16[256,2048]{1,0:T(8,128)(2,1)}, u32[]{:S(2)}, u32[]{:S(2)}) %collective-permute-start.3) | collective-permute-done | bytes 1048608 | tf_op jit(solution)/shard_map/ppermute | solution.py:563
  28.1 1.5 collective-permute-start.4
  29.7 20.7 %collective-permute-done.1.oth = bf16[256,2048]{1,0:T(8,128)(2,1)S(1)} collective-permute-done((bf16[256,2048]{1,0:T(8,128)(2,1)}, bf16[256,2048]{1,0:T(8,128)(2,1)S(1)}, u32[]{:S(2)}, u32[]{:S(2)}) %collective-permute-start.1) | collective-permute-done | bytes 1048608 | tf_op jit(solution)/shard_map/ppermute | solution.py:563
  51.4 6.7 %project_kv.3 = (bf16[2,256,256]{2,1,0:T(8,128)(2,1)S(1)}, bf16[2,256,256]{2,1,0:T(8,128)(2,1)}) custom-call(s32[16]{0:T(128)S(1)} %concatenate.33.ids.flags, bf16[512,2048]{1,0:T(8,128)(2,1)S(1)} %bitcast.54, bf16[512,2048]{1,0:T(8,128)(2,1)} %collective-permute-done.own_s, bf16[256,2048]{1,0:T(8,128)(2,1)} %collective-permute-done.3.oth, ...), custom_call_target="tpu_custom_call" | custom-call | flops 2147483648 | bytes 8388608 | tf_op jit(solution)/shard_map/project_kv/pallas_call | solution.py:63
  58.9 10.0 %project_q.2 = (bf16[2,8,512,128]{3,2,1,0:T(8,128)(2,1)}, bf16[2,256,768]{2,1,0:T(8,128)(2,1)}) custom-call(s32[16]{0:T(128)} %copy-done.18, bf16[512,2048]{1,0:T(8,128)(2,1)} %bitcast.52, bf16[512,2048]{1,0:T(8,128)(2,1)} %collective-permute-done.own_s, bf16[256,2048]{1,0:T(8,128)(2,1)} %collective-permute-done.3.oth, ...), custom_call_target="tpu_custom_call" | custom-call | flops 4294967296 | bytes 12582912 | tf_op jit(solution)/shard_map/project_q/pallas_call | solution.py:160
  68.9 23.1 %copy.12 = bf16[128,128,4,256]{3,1,0,2:T(8,128)(2,1)} copy(bf16[128,128,4,256]{3,2,1,0:T(4,128)(2,1)} %param.8) | data formatting | bytes 67108864 | tf_op args[2]
  92.1 5.8 %project_kv.2 = (bf16[2,256,256]{2,1,0:T(8,128)(2,1)S(1)}, bf16[2,256,256]{2,1,0:T(8,128)(2,1)S(1)}) custom-call(s32[16]{0:T(128)S(1)} %copy-done.19, bf16[512,2048]{1,0:T(8,128)(2,1)S(1)} %bitcast.55, bf16[512,2048]{1,0:T(8,128)(2,1)} %collective-permute-done.own_s, bf16[256,2048]{1,0:T(8,128)(2,1)S(1)} %collective-permute-done.1.oth, ...), custom_call_target="tpu_custom_call" | custom-call | flops 2147483648 | bytes 8388608 | tf_op jit(solution)/shard_map/project_kv/pallas_call | solution.py:63
  98.7 5.4 %cache_attention.2 = (f32[2,256,1024]{2,1,0:T(8,128)S(1)}, f32[2,256,1024]{2,1,0:T(8,128)S(1)}) custom-call(s32[16]{0:T(128)S(1)} %copy-done.19, s32[128]{0:T(128)S(1)} %copy-done.21, bf16[4,128,128,256]{3,2,1,0:T(8,128)(2,1)} %bitcast.62, bf16[2,8,512,128]{3,2,1,0:T(8,128)(2,1)S(1)} %copy-done.2, bf16[2,256,256]{2,1,0:T(8,128)(2,1)S(1)} %copy-done.9, ...), custom_call_target="tpu_custom_call" | custom-call | flops 1073741824 | bytes 16777216 | tf_op jit(solution)/shard_map/cache_attention/pallas_call | solution.py:289
  105.5 10.1 %project_q.3 = (bf16[2,8,512,128]{3,2,1,0:T(8,128)(2,1)}, bf16[2,256,768]{2,1,0:T(8,128)(2,1)}) custom-call(s32[16]{0:T(128)} %copy-done.18, bf16[512,2048]{1,0:T(8,128)(2,1)} %bitcast.53, bf16[512,2048]{1,0:T(8,128)(2,1)} %collective-permute-done.own_s, bf16[256,2048]{1,0:T(8,128)(2,1)} %copy-done.5, ...), custom_call_target="tpu_custom_call", output_to_operand_aliasing={{0}: (9, {})} | custom-call | flops 4294967296 | bytes 12582912 | tf_op jit(solution)/shard_map/project_q/pallas_call | solution.py:160
  116.0 19.6 %collective-permute-start.13 = (bf16[2,256,256]{2,1,0:T(8,128)(2,1)}, bf16[2,256,256]{2,1,0:T(8,128)(2,1)S(1)}, u32[]{:S(2)}, u32[]{:S(2)}) collective-permute-start(bf16[2,256,256]{2,1,0:T(8,128)(2,1)} %get-tuple-element.22.kv1.refs_2_), channel_id=1, source_target_pairs={{0,16},{1,17},{2,18},{3,19},{4,20},{5,21},{6,22},{7,23},{8,24},{9,... | collective-permute-start | bytes 786440 | tf_op jit(solution)/shard_map/ppermute | solution.py:574
  137.6 3.8 collective-permute-done.13
  141.4 2.1 collective-permute-start.14
  143.6 3.3 collective-permute-done.5
  146.9 2.3 collective-permute-start.6
  150.1 1.8 collective-permute-start.23
  151.9 1.6 copy-done.3
  154.6 5.2 %cache_attention.3 = (f32[2,256,1024]{2,1,0:T(8,128)S(1)}, f32[2,256,1024]{2,1,0:T(8,128)}) custom-call(s32[16]{0:T(128)S(1)} %copy-done.20, s32[128]{0:T(128)S(1)} %copy-done.21, bf16[4,128,128,256]{3,2,1,0:T(8,128)(2,1)} %bitcast.63, bf16[2,8,512,128]{3,2,1,0:T(8,128)(2,1)S(1)} %copy-done.3, bf16[2,256,256]{2,1,0:T(8,128)(2,1)S(1)} %copy-done.7, ...), custom_call_target="tpu_custom_call" | custom-call | flops 1073741824 | bytes 16777216 | tf_op jit(solution)/shard_map/cache_attention/pallas_call | solution.py:289
  161.3 16.9 %collective-permute-start.15 = (bf16[2,256,256]{2,1,0:T(8,128)(2,1)S(1)}, bf16[2,256,256]{2,1,0:T(8,128)(2,1)}, u32[]{:S(2)}, u32[]{:S(2)}) collective-permute-start(bf16[2,256,256]{2,1,0:T(8,128)(2,1)S(1)} %collective-permute-done.14), channel_id=1, source_target_pairs={{0,4},{2,6},{4,8},{6,10},{8,12},{10,14},{12,28},{14,30},{28,24},{3... | collective-permute-start | bytes 786440 | tf_op jit(solution)/shard_map/ppermute | solution.py:578
  179.7 4.9 %collective-permute-done.10 = bf16[2,256,256]{2,1,0:T(8,128)(2,1)} collective-permute-done((bf16[2,256,256]{2,1,0:T(8,128)(2,1)S(1)}, bf16[2,256,256]{2,1,0:T(8,128)(2,1)}, u32[]{:S(2)}, u32[]{:S(2)}) %collective-permute-start.10) | collective-permute-done | bytes 262176 | tf_op jit(solution)/shard_map/ppermute | solution.py:580
  186.0 4.1 collective-permute-done.19
  191.8 3.6 collective-permute-done.11
  197.3 3.5 collective-permute-done.20
  202.9 4.7 collective-permute-done.17
  209.5 129.0 %prompt_attention.2 = (f32[2,8,512,128]{3,2,1,0:T(8,128)}, f32[2,8,128,128]{3,2,1,0:T(8,128)S(1)}) custom-call(s32[16]{0:T(128)S(1)} %copy-done.20, bf16[2,8,512,128]{3,2,1,0:T(8,128)(2,1)S(1)} %copy-done.4, bf16[2,256,256]{2,1,0:T(8,128)(2,1)S(1)} %copy-done.9, bf16[2,256,256]{2,1,0:T(8,128)(2,1)} %get-tuple-element.22.kv1.refs_2_, ...), custom_call_target="tpu_custom_call" | custom-call | flops 8589934592 | bytes 16777216 | tf_op jit(solution)/shard_map/prompt_attention/pallas_call | solution.py:486
  338.5 2.5 pad_maximum_fusion.refs_13_
  341.0 4.9 %pad_maximum_fusion.1.refs_14_ = f32[2,512,1024]{2,1,0:T(8,128)} fusion(f32[2,256,1024]{2,1,0:T(8,128)} %collective-permute-done.24, f32[2,256,1024]{2,1,0:T(8,128)} %collective-permute-done.23), kind=kLoop, calls=%fused_computation.2 | loop fusion | flops 1048576 | bytes 8388608 | tf_op jit(solution)/shard_map/concatenate | solution.py:592
  346.1 120.0 %prompt_attention.3 = bf16[1024,1024]{1,0:T(8,128)(2,1)} custom-call(s32[16]{0:T(128)S(1)} %copy-done.20, bf16[2,8,512,128]{3,2,1,0:T(8,128)(2,1)} %get-tuple-element.24.refs_0_.q, bf16[2,256,256]{2,1,0:T(8,128)(2,1)S(1)} %copy-done.7, bf16[2,256,256]{2,1,0:T(8,128)(2,1)S(1)} %copy-done.15, bf16[512,256]{1,0:T(8,128)(2,1)S(1)} %bitcast.56, ...), custom_call_target="tpu_custom_call" | custom-call | flops 8589934592 | bytes 16777216 | tf_op jit(solution)/shard_map/prompt_attention/pallas_call | solution.py:486
  466.1 1.7 select_bitcast_fusion
  467.8 5.4 %collective-permute-start.26 = (bf16[512,1024]{1,0:T(8,128)(2,1)S(1)}, bf16[512,1024]{1,0:T(8,128)(2,1)S(1)}, u32[]{:S(2)}, u32[]{:S(2)}) collective-permute-start(bf16[512,1024]{1,0:T(8,128)(2,1)S(1)} %get-tuple-element.34), channel_id=1, source_target_pairs={{0,2},{2,0},{4,6},{6,4},{8,10},{10,8},{12,14},{14,12},{1,3},{3,1},... | collective-permute-start | bytes 3145736 | tf_op jit(solution)/shard_map/ppermute | solution.py:560
  473.2 2.3 collective-permute-done.26
  475.5 2.1 maximum_select_fusion
  (107 shorter events, 22.6 us)
Async XLA Ops:
  0.0 51.4 %copy-start = (bf16[1,512,2048]{2,1,0:T(8,128)(2,1)S(1)}, bf16[1,512,2048]{2,1,0:T(8,128)(2,1)}, u32[]{:S(2)}) copy-start(bf16[1,512,2048]{2,1,0:T(8,128)(2,1)} %param.6) | copy-start | bytes 6291460
  0.0 51.4 %collective-permute-start = (bf16[512,2048]{1,0:T(8,128)(2,1)}, bf16[512,2048]{1,0:T(8,128)(2,1)}, u32[]{:S(2)}, u32[]{:S(2)}) collective-permute-start(bf16[512,2048]{1,0:T(8,128)(2,1)} %bitcast.51), channel_id=1, source_target_pairs={{0,2},{2,0},{4,6},{6,4},{8,10},{10,8},{12,14},{14,12},{1,3},{3,1},... | collective-permute-start | bytes 6291464 | tf_op jit(solution)/shard_map/ppermute | solution.py:560
  3.4 24.7 %collective-permute-start.3 = (bf16[256,2048]{1,0:T(8,128)(2,1)S(1)}, bf16[256,2048]{1,0:T(8,128)(2,1)}, u32[]{:S(2)}, u32[]{:S(2)}) collective-permute-start(bf16[256,2048]{1,0:T(8,128)(2,1)S(1)} %get-tuple-element.35), channel_id=1, source_target_pairs={{0,1},{1,0},{2,3},{3,2},{4,5},{5,4},{6,7},{7,6},{8,9},{9,8},{10,11... | collective-permute-start | bytes 3145736 | tf_op jit(solution)/shard_map/ppermute | solution.py:563
  3.6 46.8 %collective-permute-start.1 = (bf16[256,2048]{1,0:T(8,128)(2,1)}, bf16[256,2048]{1,0:T(8,128)(2,1)S(1)}, u32[]{:S(2)}, u32[]{:S(2)}) collective-permute-start(bf16[256,2048]{1,0:T(8,128)(2,1)} %get-tuple-element.36), channel_id=1, source_target_pairs={{0,1},{1,0},{2,3},{3,2},{4,5},{5,4},{6,7},{7,6},{8,9},{9,8},{10,11... | collective-permute-start | bytes 3145736 | tf_op jit(solution)/shard_map/ppermute | solution.py:563
  28.1 23.3 %collective-permute-start.4 = (bf16[256,2048]{1,0:T(8,128)(2,1)}, bf16[256,2048]{1,0:T(8,128)(2,1)}, u32[]{:S(2)}, u32[]{:S(2)}) collective-permute-start(bf16[256,2048]{1,0:T(8,128)(2,1)} %collective-permute-done.3.oth), channel_id=1, source_target_pairs={{0,2},{2,0},{4,6},{6,4},{8,10},{10,8},{12,14},{14,12},{1,3},{3,1},... | collective-permute-start | bytes 3145736 | tf_op jit(solution)/shard_map/ppermute | solution.py:560
  50.5 41.6 %collective-permute-start.2 = (bf16[256,2048]{1,0:T(8,128)(2,1)S(1)}, bf16[256,2048]{1,0:T(8,128)(2,1)}, u32[]{:S(2)}, u32[]{:S(2)}) collective-permute-start(bf16[256,2048]{1,0:T(8,128)(2,1)S(1)} %collective-permute-done.1.oth), channel_id=1, source_target_pairs={{0,2},{2,0},{4,6},{6,4},{8,10},{10,8},{12,14},{14,12},{1,3},{3,1},... | collective-permute-start | bytes 3145736 | tf_op jit(solution)/shard_map/ppermute | solution.py:560
  68.8 29.8 %collective-permute-start.21 = (bf16[2,256,768]{2,1,0:T(8,128)(2,1)}, bf16[2,256,768]{2,1,0:T(8,128)(2,1)}, u32[]{:S(2)}, u32[]{:S(2)}) collective-permute-start(bf16[2,256,768]{2,1,0:T(8,128)(2,1)} %get-tuple-element.27), channel_id=1, source_target_pairs={{0,2},{2,0},{4,6},{6,4},{8,10},{10,8},{12,14},{14,12},{1,3},{3,1},... | collective-permute-start | bytes 2359304 | tf_op jit(solution)/shard_map/ppermute | solution.py:560
  105.5 46.4 %copy-start.20 = (s32[16]{0:T(128)S(1)}, s32[16]{0:T(128)}, u32[]{:S(2)}) copy-start(s32[16]{0:T(128)} %copy-done.18) | copy-start | bytes 196
  115.5 33.7 %collective-permute-start.22 = (bf16[2,256,768]{2,1,0:T(8,128)(2,1)}, bf16[2,256,768]{2,1,0:T(8,128)(2,1)S(1)}, u32[]{:S(2)}, u32[]{:S(2)}) collective-permute-start(bf16[2,256,768]{2,1,0:T(8,128)(2,1)} %get-tuple-element.29), channel_id=1, source_target_pairs={{0,2},{2,0},{4,6},{6,4},{8,10},{10,8},{12,14},{14,12},{1,3},{3,1},... | collective-permute-start | bytes 2359304 | tf_op jit(solution)/shard_map/ppermute | solution.py:560
  116.0 25.4 %collective-permute-start.13 = (bf16[2,256,256]{2,1,0:T(8,128)(2,1)}, bf16[2,256,256]{2,1,0:T(8,128)(2,1)S(1)}, u32[]{:S(2)}, u32[]{:S(2)}) collective-permute-start(bf16[2,256,256]{2,1,0:T(8,128)(2,1)} %get-tuple-element.22.kv1.refs_2_), channel_id=1, source_target_pairs={{0,16},{1,17},{2,18},{3,19},{4,20},{5,21},{6,22},{7,23},{8,24},{9,... | collective-permute-start | bytes 786440 | tf_op jit(solution)/shard_map/ppermute | solution.py:574
  135.6 11.3 %collective-permute-start.5 = (bf16[2,256,256]{2,1,0:T(8,128)(2,1)S(1)}, bf16[2,256,256]{2,1,0:T(8,128)(2,1)S(1)}, u32[]{:S(2)}, u32[]{:S(2)}) collective-permute-start(bf16[2,256,256]{2,1,0:T(8,128)(2,1)S(1)} %copy-done.15), channel_id=1, source_target_pairs={{0,16},{1,17},{2,18},{3,19},{4,20},{5,21},{6,22},{7,23},{8,24},{9,... | collective-permute-start | bytes 786440 | tf_op jit(solution)/shard_map/ppermute | solution.py:574
  137.1 24.1 %collective-permute-start.25 = (f32[512]{0:T(512)S(1)}, f32[512]{0:T(512)S(1)}, u32[]{:S(2)}, u32[]{:S(2)}) collective-permute-start(f32[512]{0:T(512)S(1)} %convert_element_type.20), channel_id=1, source_target_pairs={{0,2},{2,0},{4,6},{6,4},{8,10},{10,8},{12,14},{14,12},{1,3},{3,1},... | collective-permute-start | bytes 6152 | tf_op jit(solution)/shard_map/ppermute | solution.py:560
  141.4 19.8 %collective-permute-start.14 = (bf16[2,256,256]{2,1,0:T(8,128)(2,1)S(1)}, bf16[2,256,256]{2,1,0:T(8,128)(2,1)S(1)}, u32[]{:S(2)}, u32[]{:S(2)}) collective-permute-start(bf16[2,256,256]{2,1,0:T(8,128)(2,1)S(1)} %broadcast_select_fusion.1), channel_id=1, source_target_pairs={{0,4},{2,6},{4,8},{6,10},{8,12},{10,14},{12,28},{14,30},{28,24},{3... | collective-permute-start | bytes 786440 | tf_op jit(solution)/shard_map/ppermute | solution.py:578
  143.6 17.7 %collective-permute-start.18 = (bf16[2,256,256]{2,1,0:T(8,128)(2,1)S(1)}, bf16[2,256,256]{2,1,0:T(8,128)(2,1)S(1)}, u32[]{:S(2)}, u32[]{:S(2)}) collective-permute-start(bf16[2,256,256]{2,1,0:T(8,128)(2,1)S(1)} %broadcast_select_fusion.1), channel_id=1, source_target_pairs={{0,16},{2,18},{4,0},{6,2},{8,4},{10,6},{12,8},{14,10},{28,12},{30,... | collective-permute-start | bytes 786440 | tf_op jit(solution)/shard_map/ppermute | solution.py:580
  146.9 32.0 %collective-permute-start.6 = (bf16[2,256,256]{2,1,0:T(8,128)(2,1)S(1)}, bf16[2,256,256]{2,1,0:T(8,128)(2,1)}, u32[]{:S(2)}, u32[]{:S(2)}) collective-permute-start(bf16[2,256,256]{2,1,0:T(8,128)(2,1)S(1)} %broadcast_select_fusion.2), channel_id=1, source_target_pairs={{0,4},{2,6},{4,8},{6,10},{8,12},{10,14},{12,28},{14,30},{28,24},{3... | collective-permute-start | bytes 786440 | tf_op jit(solution)/shard_map/ppermute | solution.py:578
  150.1 190.9 %collective-permute-start.23 = (f32[2,256,1024]{2,1,0:T(8,128)}, f32[2,256,1024]{2,1,0:T(8,128)}, u32[]{:S(2)}, u32[]{:S(2)}) collective-permute-start(f32[2,256,1024]{2,1,0:T(8,128)} %copy-done.22), channel_id=1, source_target_pairs={{0,2},{2,0},{4,6},{6,4},{8,10},{10,8},{12,14},{14,12},{1,3},{3,1},... | collective-permute-start | bytes 6291464 | tf_op jit(solution)/shard_map/ppermute | solution.py:560
  154.6 53.0 %copy-start.4 = (bf16[2,8,512,128]{3,2,1,0:T(8,128)(2,1)S(1)}, bf16[2,8,512,128]{3,2,1,0:T(8,128)(2,1)}, u32[]{:S(2)}) copy-start(bf16[2,8,512,128]{3,2,1,0:T(8,128)(2,1)} %get-tuple-element.24.refs_0_.q) | copy-start | bytes 6291460
  161.2 179.8 %collective-permute-start.24 = (f32[2,256,1024]{2,1,0:T(8,128)}, f32[2,256,1024]{2,1,0:T(8,128)}, u32[]{:S(2)}, u32[]{:S(2)}) collective-permute-start(f32[2,256,1024]{2,1,0:T(8,128)} %get-tuple-element.32), channel_id=1, source_target_pairs={{0,2},{2,0},{4,6},{6,4},{8,10},{10,8},{12,14},{14,12},{1,3},{3,1},... | collective-permute-start | bytes 6291464 | tf_op jit(solution)/shard_map/ppermute | solution.py:560
  161.2 23.3 %collective-permute-start.10 = (bf16[2,256,256]{2,1,0:T(8,128)(2,1)S(1)}, bf16[2,256,256]{2,1,0:T(8,128)(2,1)}, u32[]{:S(2)}, u32[]{:S(2)}) collective-permute-start(bf16[2,256,256]{2,1,0:T(8,128)(2,1)S(1)} %broadcast_select_fusion.2), channel_id=1, source_target_pairs={{0,16},{2,18},{4,0},{6,2},{8,4},{10,6},{12,8},{14,10},{28,12},{30,... | collective-permute-start | bytes 786440 | tf_op jit(solution)/shard_map/ppermute | solution.py:580
  161.3 24.4 %collective-permute-start.15 = (bf16[2,256,256]{2,1,0:T(8,128)(2,1)S(1)}, bf16[2,256,256]{2,1,0:T(8,128)(2,1)}, u32[]{:S(2)}, u32[]{:S(2)}) collective-permute-start(bf16[2,256,256]{2,1,0:T(8,128)(2,1)S(1)} %collective-permute-done.14), channel_id=1, source_target_pairs={{0,4},{2,6},{4,8},{6,10},{8,12},{10,14},{12,28},{14,30},{28,24},{3... | collective-permute-start | bytes 786440 | tf_op jit(solution)/shard_map/ppermute | solution.py:578
  179.0 11.2 %collective-permute-start.19 = (bf16[2,256,256]{2,1,0:T(8,128)(2,1)S(1)}, bf16[2,256,256]{2,1,0:T(8,128)(2,1)}, u32[]{:S(2)}, u32[]{:S(2)}) collective-permute-start(bf16[2,256,256]{2,1,0:T(8,128)(2,1)S(1)} %collective-permute-done.18), channel_id=1, source_target_pairs={{0,16},{2,18},{4,0},{6,2},{8,4},{10,6},{12,8},{14,10},{28,12},{30,... | collective-permute-start | bytes 786440 | tf_op jit(solution)/shard_map/ppermute | solution.py:580
  184.6 6.9 %collective-permute-start.7 = (bf16[2,256,256]{2,1,0:T(8,128)(2,1)}, bf16[2,256,256]{2,1,0:T(8,128)(2,1)}, u32[]{:S(2)}, u32[]{:S(2)}) collective-permute-start(bf16[2,256,256]{2,1,0:T(8,128)(2,1)} %collective-permute-done.6), channel_id=1, source_target_pairs={{0,4},{2,6},{4,8},{6,10},{8,12},{10,14},{12,28},{14,30},{28,24},{3... | collective-permute-start | bytes 786440 | tf_op jit(solution)/shard_map/ppermute | solution.py:578
  185.7 9.7 %collective-permute-start.11 = (bf16[2,256,256]{2,1,0:T(8,128)(2,1)}, bf16[2,256,256]{2,1,0:T(8,128)(2,1)}, u32[]{:S(2)}, u32[]{:S(2)}) collective-permute-start(bf16[2,256,256]{2,1,0:T(8,128)(2,1)} %collective-permute-done.10), channel_id=1, source_target_pairs={{0,16},{2,18},{4,0},{6,2},{8,4},{10,6},{12,8},{14,10},{28,12},{30,... | collective-permute-start | bytes 786440 | tf_op jit(solution)/shard_map/ppermute | solution.py:580
  190.2 6.8 %collective-permute-start.16 = (bf16[2,256,256]{2,1,0:T(8,128)(2,1)}, bf16[2,256,256]{2,1,0:T(8,128)(2,1)}, u32[]{:S(2)}, u32[]{:S(2)}) collective-permute-start(bf16[2,256,256]{2,1,0:T(8,128)(2,1)} %collective-permute-done.15), channel_id=1, source_target_pairs={{0,4},{2,6},{4,8},{6,10},{8,12},{10,14},{12,28},{14,30},{28,24},{3... | collective-permute-start | bytes 786440 | tf_op jit(solution)/shard_map/ppermute | solution.py:578
  191.4 9.4 %collective-permute-start.20 = (bf16[2,256,256]{2,1,0:T(8,128)(2,1)}, bf16[2,256,256]{2,1,0:T(8,128)(2,1)}, u32[]{:S(2)}, u32[]{:S(2)}) collective-permute-start(bf16[2,256,256]{2,1,0:T(8,128)(2,1)} %collective-permute-done.19), channel_id=1, source_target_pairs={{0,16},{2,18},{4,0},{6,2},{8,4},{10,6},{12,8},{14,10},{28,12},{30,... | collective-permute-start | bytes 786440 | tf_op jit(solution)/shard_map/ppermute | solution.py:580
  195.4 6.6 %collective-permute-start.8 = (bf16[2,256,256]{2,1,0:T(8,128)(2,1)}, bf16[2,256,256]{2,1,0:T(8,128)(2,1)}, u32[]{:S(2)}, u32[]{:S(2)}) collective-permute-start(bf16[2,256,256]{2,1,0:T(8,128)(2,1)} %collective-permute-done.7), channel_id=1, source_target_pairs={{0,4},{2,6},{4,8},{6,10},{8,12},{10,14},{12,28},{14,30},{28,24},{3... | collective-permute-start | bytes 786440 | tf_op jit(solution)/shard_map/ppermute | solution.py:578
  197.0 10.7 %collective-permute-start.17 = (bf16[2,256,256]{2,1,0:T(8,128)(2,1)}, bf16[2,256,256]{2,1,0:T(8,128)(2,1)}, u32[]{:S(2)}, u32[]{:S(2)}) collective-permute-start(bf16[2,256,256]{2,1,0:T(8,128)(2,1)} %collective-permute-done.16), channel_id=1, source_target_pairs={{0,4},{2,6},{4,8},{6,10},{8,12},{10,14},{12,28},{14,30},{28,24},{3... | collective-permute-start | bytes 786440 | tf_op jit(solution)/shard_map/ppermute | solution.py:578
  200.9 145.0 %collective-permute-start.12 = (bf16[2,256,256]{2,1,0:T(8,128)(2,1)}, bf16[2,256,256]{2,1,0:T(8,128)(2,1)S(1)}, u32[]{:S(2)}, u32[]{:S(2)}) collective-permute-start(bf16[2,256,256]{2,1,0:T(8,128)(2,1)} %collective-permute-done.11), channel_id=1, source_target_pairs={{0,16},{2,18},{4,0},{6,2},{8,4},{10,6},{12,8},{14,10},{28,12},{30,... | collective-permute-start | bytes 786440 | tf_op jit(solution)/shard_map/ppermute | solution.py:580
  202.0 143.9 %collective-permute-start.9 = (bf16[2,256,256]{2,1,0:T(8,128)(2,1)}, bf16[2,256,256]{2,1,0:T(8,128)(2,1)S(1)}, u32[]{:S(2)}, u32[]{:S(2)}) collective-permute-start(bf16[2,256,256]{2,1,0:T(8,128)(2,1)} %collective-permute-done.8), channel_id=1, source_target_pairs={{0,4},{2,6},{4,8},{6,10},{8,12},{10,14},{12,28},{14,30},{28,24},{3... | collective-permute-start | bytes 786440 | tf_op jit(solution)/shard_map/ppermute | solution.py:578
  209.5 129.0 %copy-start.11 = (f32[2,256,1024]{2,1,0:T(8,128)S(1)}, f32[2,256,1024]{2,1,0:T(8,128)}, u32[]{:S(2)}) copy-start(f32[2,256,1024]{2,1,0:T(8,128)} %copy-done.10) | copy-start | bytes 6291460
  209.5 129.0 %copy-start.13 = (f32[2,256,1024]{2,1,0:T(8,128)S(1)}, f32[2,256,1024]{2,1,0:T(8,128)}, u32[]{:S(2)}) copy-start(f32[2,256,1024]{2,1,0:T(8,128)} %copy-done.12) | copy-start | bytes 6291460
  467.8 7.7 %collective-permute-start.26 = (bf16[512,1024]{1,0:T(8,128)(2,1)S(1)}, bf16[512,1024]{1,0:T(8,128)(2,1)S(1)}, u32[]{:S(2)}, u32[]{:S(2)}) collective-permute-start(bf16[512,1024]{1,0:T(8,128)(2,1)S(1)} %get-tuple-element.34), channel_id=1, source_target_pairs={{0,2},{2,0},{4,6},{6,4},{8,10},{10,8},{12,14},{14,12},{1,3},{3,1},... | collective-permute-start | bytes 3145736 | tf_op jit(solution)/shard_map/ppermute | solution.py:560
  (24 other events, 295.7 us)
